TPU v7x, 512 devices: a whole 4x8x8 slice. The times are simulated.
512 devices in a mesh: req: 16 (over y, core), ctx: 32 (over z, x).
Axes of the slice: x: 4, y: 8, z: 8, core: 2. Of those that a mesh axis runs over, the one named last changes fastest.
Arguments:
- latent_cache: bfloat16 [917504, 512], P(('req', 'ctx')), parts along dimension 0, may hold values from -6 to 6
- rope_cache: bfloat16 [917504, 64], P(('req', 'ctx')), parts along dimension 0, may hold values from -6 to 6
- lengths: int32 [32], P('req'), parts along dimension 0, may hold values from 1 to 35840, 57344 in all
- target_shard: int32 [917504], P(('req', 'ctx')), parts along dimension 0, may hold values from 0 to 31, as said below
- query_nope: bfloat16 [2, 32, 64, 128], P(None, 'req', 'ctx'), parts along dimension 1, may hold values from -12 to 12
- query_rope: bfloat16 [2, 32, 64, 64], P(None, 'req', 'ctx'), parts along dimension 1, may hold values from -400 to 400
- new_latent: bfloat16 [2, 32, 512], P(None, 'req'), parts along dimension 1, may hold values from -6 to 6
- new_rope: bfloat16 [2, 32, 64], P(None, 'req'), parts along dimension 1, may hold values from -6 to 6
- key_absorb: bfloat16 [64, 128, 512], P('ctx'), may hold values from -0.5 to 0.5
- value_up: bfloat16 [64, 512, 128], P('ctx'), may hold values from -0.25 to 0.25
Outputs:
- attention: bfloat16 [2, 32, 64, 128], P(None, 'req', 'ctx'), parts along dimension 1
- latent_decode: bfloat16 [917504, 512], P(('req', 'ctx')), parts along dimension 0
- rope_decode: bfloat16 [917504, 64], P(('req', 'ctx')), parts along dimension 0
There are 16 independent parts, one for each index of `req`. A program takes and returns all parts, laid end to end along the dimension named above; an argument that names none is the same for every part. Nothing has to cross between parts.
Inputs may be any that keep to these rules, and one draw needn't show every extreme that they name: `target_shard`: each aligned block of 1792 positions names every shard exactly 56 times.
All inputs are finite; a program needn't handle non-finite values.
Results may differ from a plain program's by a relative error of at most 0.019.
Values may be sent and summed in bfloat16 or wider, within the bound.
A program may use at most 128 MiB of HBM per device.

v0:
```python
import math

import jax
import jax.numpy as jnp
from jax import lax
from jax.sharding import PartitionSpec as P

NEG = -1e30


def joined(value, axis, join):
    pieces = jax.tree.map(lambda part: lax.all_gather(part, axis), value)
    head = jax.tree.map(lambda part: part[0], pieces)
    tail = jax.tree.map(lambda part: part[1:], pieces)
    so_far, _ = lax.scan(lambda so_far, slab: (join(so_far, slab), None), head, tail)
    return so_far


def request_of(positions, lengths):
    bounds = jnp.cumsum(lengths)[:-1]
    return jnp.sum((positions[:, None] >= bounds[None, :]).astype(jnp.int32), axis=1)


def contract(left, right):
    return lax.dot_general(
        left, right, (((1,), (1,)), ((), ())), preferred_element_type=jnp.float32
    )


def partial_attention(
    query_latent,
    query_rope,
    row_request,
    cache_latent,
    cache_rope,
    token_request,
    fresh_latent,
    fresh_rope,
    own_fresh,
    score_scale,
    request_count,
):
    step_count, row_count = (query_latent.shape[0], query_latent.shape[1])
    flat_latent = query_latent.reshape(step_count * row_count, -1)
    flat_rope = query_rope.reshape(step_count * row_count, -1)
    scores = (contract(flat_latent, cache_latent) + contract(flat_rope, cache_rope)) * score_scale
    scores = scores.reshape(step_count, row_count, -1)
    fresh_scores = (
        contract(flat_latent, fresh_latent) + contract(flat_rope, fresh_rope)
    ) * score_scale
    fresh_scores = fresh_scores.reshape(step_count, row_count, -1)
    usable = jnp.broadcast_to(
        row_request[None, :, None] == token_request[None, None, :], scores.shape
    )
    fresh_index = jnp.arange(fresh_latent.shape[0], dtype=jnp.int32)
    step_index = jnp.arange(step_count, dtype=jnp.int32)
    fresh_usable = (
        (fresh_index[None, None, :] // request_count <= step_index[:, None, None])
        & (fresh_index[None, None, :] % request_count == row_request[None, :, None])
        & own_fresh
    )
    masked = jnp.where(usable, scores, NEG)
    fresh_masked = jnp.where(fresh_usable, fresh_scores, NEG)
    row_peak = jnp.maximum(jnp.max(masked, axis=-1), jnp.max(fresh_masked, axis=-1))
    weights = jnp.where(usable, jnp.exp(masked - row_peak[..., None]), 0.0)
    fresh_weights = jnp.where(fresh_usable, jnp.exp(fresh_masked - row_peak[..., None]), 0.0)
    totals = jnp.sum(weights, axis=-1) + jnp.sum(fresh_weights, axis=-1)
    weighted = jnp.dot(
        weights.astype(jnp.bfloat16).reshape(step_count * row_count, -1),
        cache_latent,
        preferred_element_type=jnp.float32,
    )
    weighted = weighted + jnp.dot(
        fresh_weights.astype(jnp.bfloat16).reshape(step_count * row_count, -1),
        fresh_latent,
        preferred_element_type=jnp.float32,
    )
    return (row_peak, totals, weighted.reshape(step_count, row_count, -1))


def combine_parts(first, second):
    row_peak = jnp.maximum(first[0], second[0])
    factor_a = jnp.exp(first[0] - row_peak)
    factor_b = jnp.exp(second[0] - row_peak)
    return (
        row_peak,
        first[1] * factor_a + second[1] * factor_b,
        first[2] * factor_a[..., None] + second[2] * factor_b[..., None],
    )


def local(
    latent_cache,
    rope_cache,
    lengths,
    target_shard,
    query_nope,
    query_rope,
    new_latent,
    new_rope,
    key_absorb,
    value_up,
):
    shards = lax.axis_size("ctx")
    own_index = lax.axis_index("ctx")
    tok_count = latent_cache.shape[0]
    per_peer = tok_count // shards
    width_lat = latent_cache.shape[1]
    width_rope = rope_cache.shape[1]
    step_count, request_count, heads_dev = (
        query_nope.shape[0],
        query_nope.shape[1],
        query_nope.shape[2],
    )
    head_count = heads_dev * shards
    row_count = request_count * head_count
    score_scale = 1.0 / math.sqrt(query_nope.shape[3] + width_rope)
    positions = own_index * tok_count + jnp.arange(tok_count, dtype=jnp.int32)
    token_request = request_of(positions, lengths)
    send_order = jnp.argsort(target_shard, stable=True)
    sent_latent = latent_cache[send_order].reshape(shards, per_peer, width_lat)
    sent_rope = rope_cache[send_order].reshape(shards, per_peer, width_rope)
    query_latent = jnp.einsum(
        "srhn,hnl->srhl", query_nope, key_absorb, preferred_element_type=jnp.float32
    ).astype(jnp.bfloat16)
    all_latent, all_rope = (
        lax.all_gather(query_latent, "ctx", axis=2, tiled=True),
        lax.all_gather(query_rope, "ctx", axis=2, tiled=True),
    )
    all_latent = all_latent.reshape(step_count, row_count, width_lat)
    all_rope = all_rope.reshape(step_count, row_count, width_rope)
    row_request = jnp.arange(row_count, dtype=jnp.int32) // head_count
    fresh_latent = new_latent.reshape(step_count * request_count, width_lat)
    fresh_rope = new_rope.reshape(step_count * request_count, width_rope)
    own_fresh = own_index == 0
    req_flags = token_request.astype(jnp.bfloat16)[send_order].reshape(shards, per_peer)
    got_latent, got_rope, got_flags = (
        lax.all_to_all(sent_latent, "ctx", split_axis=0, concat_axis=0, tiled=True),
        lax.all_to_all(sent_rope, "ctx", split_axis=0, concat_axis=0, tiled=True),
        lax.all_to_all(req_flags, "ctx", split_axis=0, concat_axis=0, tiled=True),
    )
    latent_decode = got_latent.reshape(tok_count, width_lat)
    rope_decode = got_rope.reshape(tok_count, width_rope)
    thresholds = jnp.arange(1, request_count, dtype=jnp.float32) - 0.5
    decode_request = jnp.sum(
        (got_flags.reshape(tok_count).astype(jnp.float32)[:, None] > thresholds[None, :]).astype(
            jnp.int32
        ),
        axis=1,
    )
    row_peak, totals, weighted = partial_attention(
        all_latent,
        all_rope,
        row_request,
        latent_decode,
        rope_decode,
        decode_request,
        fresh_latent,
        fresh_rope,
        own_fresh,
        score_scale,
        request_count,
    )
    row_peak, totals, weighted = joined((row_peak, totals, weighted), "ctx", combine_parts)
    whole_out = (weighted / totals[..., None]).reshape(
        step_count, request_count, head_count, width_lat
    )
    own_out = lax.dynamic_slice_in_dim(whole_out, own_index * heads_dev, heads_dev, 2)
    latent_out = own_out.astype(jnp.bfloat16)
    attention = jnp.einsum(
        "srhl,hlv->srhv", latent_out, value_up, preferred_element_type=jnp.float32
    ).astype(jnp.bfloat16)
    return (attention, latent_decode, rope_decode)


def solution(mesh):
    placed = (
        P(("req", "ctx"), None),
        P(("req", "ctx"), None),
        P("req"),
        P(("req", "ctx")),
        P(None, "req", "ctx", None),
        P(None, "req", "ctx", None),
        P(None, "req", None),
        P(None, "req", None),
        P("ctx", None, None),
        P("ctx", None, None),
    )
    return jax.shard_map(
        local,
        mesh=mesh,
        in_specs=placed,
        out_specs=(P(None, "req", "ctx", None), P(("req", "ctx"), None), P(("req", "ctx"), None)),
        check_vma=False,
    )
```

profile of v0, /device:TPU:1, one launch (start us, length us, event | category | flops | bytes accessed | tf_op | source)
XLA Modules:
  0.0 418.5 jit_solution(2122527258489085965)
XLA Ops:
  7.2 5.9 %sort.17 = (s32[1792]{0:T(1024)}, s32[1792]{0:T(1024)S(1)}) sort(s32[1792]{0:T(1024)} %param.15, s32[1792]{0:T(1024)S(1)} %iota.30), dimensions={0}, to_apply=%region_1.2 | sort | flops 19712 | bytes 28672 | tf_op jit(solution)/shard_map/jit(argsort)/sort | solution.py:120
  14.0 10.9 %gather_fusion = bf16[1792]{0:T(1024)(128)(2,1)S(1)} fusion(bf16[1792]{0:T(1024)(128)(2,1)S(1)} %convert_convert_fusion, s32[2048]{0:T(1024)S(1)} %pad_clamp_fusion), kind=kCustom, calls=%fused_computation | custom fusion | bytes 14336 | tf_op jit(solution)/shard_map/gather | solution.py:136
  25.6 13.7 %all-to-all-start = ((bf16[32,1,56]{2,1,0:T(2,128)(2,1)}), bf16[32,1,56]{2,1,0:T(2,128)(2,1)S(1)}, u32[]{:S(2)}, u32[]{:S(2)}) async-start(bf16[32,1,56]{2,1,0:T(2,128)(2,1)} %all_to_all.16), calls=%async_computation | async-start | bytes 32768 | tf_op jit(solution)/shard_map/all_to_all | solution.py:140
  39.6 3.7 gather_fusion.2
  44.3 3.5 all-to-all-done
  47.9 5.7 %all-to-all-start.2 = ((bf16[32,2,1792]{2,1,0:T(2,128)(2,1)}), bf16[32,2,1792]{2,1,0:T(2,128)(2,1)S(1)}, u32[]{:S(2)}, u32[]{:S(2)}) async-start(bf16[32,2,1792]{2,1,0:T(2,128)(2,1)} %reshape.340), calls=%async_computation.2 | async-start | bytes 458752 | tf_op jit(solution)/shard_map/all_to_all | solution.py:139
  53.6 6.1 %gather_fusion.1 = bf16[1792,512]{1,0:T(8,128)(2,1)} fusion(bf16[1792,512]{1,0:T(8,128)(2,1)S(1)} %copy-done, s32[2048]{0:T(1024)S(1)} %pad_clamp_fusion), kind=kCustom, calls=%fused_computation.1 | custom fusion | bytes 3677184 | tf_op jit(solution)/shard_map/gather | solution.py:121
  59.7 4.0 all-to-all-done.2
  63.7 5.5 %all-to-all-start.1 = ((bf16[32,56,512]{2,1,0:T(8,128)(2,1)}), bf16[32,56,512]{2,1,0:T(8,128)(2,1)}, u32[]{:S(2)}, u32[]{:S(2)}) async-start(bf16[32,56,512]{2,1,0:T(8,128)(2,1)} %bitcast.82), calls=%async_computation.1 | async-start | bytes 3670016 | tf_op jit(solution)/shard_map/all_to_all | solution.py:138
  69.3 71.1 %all_gather.18 = bf16[2,2,64,64]{3,1,0,2:T(2,128)(2,1)S(1)} all-gather(bf16[2,2,2,64]{3,1,0,2:T(2,128)(2,1)S(1)} %copy.39), channel_id=1, replica_groups=mesh['req'=16,'ctx'=32] {'ctx'}, dimensions={2}, use_global_device_ids=true | all-gather | bytes 33792 | tf_op jit(solution)/shard_map/all_gather | solution.py:128
  140.8 35.4 %all_gather.17 = bf16[2,2,64,512]{3,1,0,2:T(2,128)(2,1)S(1)} all-gather(bf16[2,2,2,512]{3,1,0,2:T(2,128)(2,1)S(1)} %fusion.7), channel_id=1, replica_groups=mesh['req'=16,'ctx'=32] {'ctx'}, dimensions={2}, use_global_device_ids=true | all-gather | bytes 270336 | tf_op jit(solution)/shard_map/all_gather | solution.py:127
  177.4 1.7 convolution_bitcast_fusion
  179.2 2.9 fusion.19
  182.7 2.1 fusion.22
  186.9 31.7 %all_gather.19 = f32[32,2,128]{2,1,0:T(2,128)S(1)} all-gather(f32[1,2,128]{2,1,0:T(2,128)S(1)} %bitcast.91), channel_id=1, replica_groups=mesh['req'=16,'ctx'=32] {'ctx'}, dimensions={0}, use_global_device_ids=true | all-gather | bytes 33792 | tf_op jit(solution)/shard_map/all_gather | solution.py:12
  218.7 34.9 %all_gather.20 = f32[32,2,128]{2,1,0:T(2,128)S(1)} all-gather(f32[1,2,128]{2,1,0:T(2,128)S(1)} %add_bitcast_fusion), channel_id=1, replica_groups=mesh['req'=16,'ctx'=32] {'ctx'}, dimensions={0}, use_global_device_ids=true | all-gather | bytes 33792 | tf_op jit(solution)/shard_map/all_gather | solution.py:12
  253.6 102.3 %all-gather.2.cloned.1.call-done = f32[32,2,128,512]{3,2,1,0:T(8,128)} async-done(((f32[1,2,128,512]{3,2,1,0:T(8,128)}), f32[32,2,128,512]{3,2,1,0:T(8,128)}) %all-gather.2.cloned.1.call-update) | async-done | bytes 16777232 | tf_op jit(solution)/shard_map/all_gather | solution.py:12
  357.0 11.8 %slice.40 = f32[31,2,128,512]{3,2,1,0:T(8,128)} slice(f32[32,2,128,512]{3,2,1,0:T(8,128)} %all-gather.2.cloned.1.call-done), slice={[1:32], [0:2], [0:128], [0:512]} | slice | bytes 32505856 | tf_op jit(solution)/shard_map/slice | solution.py:14
  368.8 39.1 %while.14 = (s32[]{:T(128)}, f32[2,128]{1,0:T(2,128)S(1)}, f32[2,128]{1,0:T(2,128)S(1)}, f32[2,128,512]{2,1,0:T(8,128)S(1)}, f32[31,2,128]{2,1,0:T(2,128)S(1)}, ...) while((s32[]{:T(128)}, f32[2,128]{1,0:T(2,128)S(1)}, f32[2,128]{1,0:T(2,128)S(1)}, ...), condition=%wide.region_7.8_spmd, body=%wide.region_6.7_spmd.sunk | while | flops 394754 | bytes 1583205 | solution.py:15
  368.8 1.2 fusion.37
  371.4 1.2 fusion.37
  372.6 1.2 fusion.37
  376.4 1.2 fusion.37
  408.8 2.8 copy.68
  (118 shorter events, 42.6 us)
Async XLA Ops:
  7.2 46.4 %copy-start = (bf16[1792,512]{1,0:T(8,128)(2,1)S(1)}, bf16[1792,512]{1,0:T(8,128)(2,1)}, u32[]{:S(2)}) copy-start(bf16[1792,512]{1,0:T(8,128)(2,1)} %param.12) | copy-start | bytes 5505028
  14.0 25.4 %copy-start.2 = (bf16[1792,64]{0,1:T(8,128)(2,1)S(1)}, bf16[1792,64]{0,1:T(8,128)(2,1)}, u32[]{:S(2)}) copy-start(bf16[1792,64]{0,1:T(8,128)(2,1)} %param.13) | copy-start | bytes 688132
  25.6 22.2 %all-to-all-start = ((bf16[32,1,56]{2,1,0:T(2,128)(2,1)}), bf16[32,1,56]{2,1,0:T(2,128)(2,1)S(1)}, u32[]{:S(2)}, u32[]{:S(2)}) async-start(bf16[32,1,56]{2,1,0:T(2,128)(2,1)} %all_to_all.16), calls=%async_computation | async-start | bytes 32768 | tf_op jit(solution)/shard_map/all_to_all | solution.py:140
  47.9 15.9 %all-to-all-start.2 = ((bf16[32,2,1792]{2,1,0:T(2,128)(2,1)}), bf16[32,2,1792]{2,1,0:T(2,128)(2,1)S(1)}, u32[]{:S(2)}, u32[]{:S(2)}) async-start(bf16[32,2,1792]{2,1,0:T(2,128)(2,1)} %reshape.340), calls=%async_computation.2 | async-start | bytes 458752 | tf_op jit(solution)/shard_map/all_to_all | solution.py:139
  63.7 5.6 %copy-start.5 = (bf16[2,2,2,64]{3,2,1,0:T(2,128)(2,1)S(1)}, bf16[2,2,2,64]{3,2,1,0:T(2,128)(2,1)}, u32[]{:S(2)}) copy-start(bf16[2,2,2,64]{3,2,1,0:T(2,128)(2,1)} %param.17) | copy-start | bytes 3076
  63.7 5.6 %copy-start.3 = (bf16[2,2,512]{2,1,0:T(2,128)(2,1)S(1)}, bf16[2,2,512]{2,1,0:T(2,128)(2,1)}, u32[]{:S(2)}) copy-start(bf16[2,2,512]{2,1,0:T(2,128)(2,1)} %param.18) | copy-start | bytes 12292
  63.7 76.9 %copy-start.1 = (bf16[2,128,512]{2,1,0:T(8,128)(2,1)S(1)}, bf16[2,128,512]{2,1,0:T(8,128)(2,1)}, u32[]{:S(2)}) copy-start(bf16[2,128,512]{2,1,0:T(8,128)(2,1)} %param.20) | copy-start | bytes 786436
  63.7 76.9 %copy-start.4 = (bf16[2,2,2,128]{3,2,1,0:T(2,128)(2,1)S(1)}, bf16[2,2,2,128]{3,2,1,0:T(2,128)(2,1)}, u32[]{:S(2)}) copy-start(bf16[2,2,2,128]{3,2,1,0:T(2,128)(2,1)} %param.16) | copy-start | bytes 6148
  63.7 112.8 %copy-start.7 = (bf16[2,2,64]{2,1,0:T(2,128)(2,1)S(1)}, bf16[2,2,64]{2,1,0:T(2,128)(2,1)}, u32[]{:S(2)}) copy-start(bf16[2,2,64]{2,1,0:T(2,128)(2,1)} %param.19) | copy-start | bytes 1540
  63.7 115.3 %all-to-all-start.1 = ((bf16[32,56,512]{2,1,0:T(8,128)(2,1)}), bf16[32,56,512]{2,1,0:T(8,128)(2,1)}, u32[]{:S(2)}, u32[]{:S(2)}) async-start(bf16[32,56,512]{2,1,0:T(8,128)(2,1)} %bitcast.82), calls=%async_computation.1 | async-start | bytes 3670016 | tf_op jit(solution)/shard_map/all_to_all | solution.py:138
  69.2 286.7 %all-gather.2.cloned.1.call-start = ((), (), s32[]{:S(2)}) async-start(), calls=%async_computation.3 | async-start | bytes 17301504 | tf_op jit(solution)/shard_map/all_gather | solution.py:12
  368.8 39.2 %copy-start.6 = (bf16[2,512,128]{2,1,0:T(8,128)(2,1)S(1)}, bf16[2,512,128]{2,1,0:T(8,128)(2,1)}, u32[]{:S(2)}) copy-start(bf16[2,512,128]{2,1,0:T(8,128)(2,1)} %param.21) | copy-start | bytes 786436
Sparse Core Ops, SparseCore 0:
  186.1 169.7 all-gather.1
where the time goes:
time: 420 us; the launch traced here: 418 us
  blocking collectives  173 us (41%)
  waiting for transfers between devices  110 us (26%)
  other arithmetic  46.2 us (11%)
  local copies, waits for them, and re-layouts  40.8 us (10%)
  starting transfers between devices  24.9 us (6%)
  between operations  14.3 us (3%)
  matrix products  8.49 us (2%)
    all_gather x1, waiting for transfers between devices, joined(): pieces = jax.tree.map(lambda part: lax.all_gather(part, axis), value)  102 us
    all_gather x1, blocking collectives, local(): lax.all_gather(query_rope, 'ctx', axis=2, tiled=True)  71.1 us
    all_gather x2, blocking collectives, joined(): pieces = jax.tree.map(lambda part: lax.all_gather(part, axis), value)  66.6 us
    add x31, other arithmetic, combine_parts(): first[2] * factor_a[..., None] + second[2] * factor_b[..., None]  37.6 us
    all_gather x1, blocking collectives, local(): lax.all_gather(query_latent, 'ctx', axis=2, tiled=True)  35.4 us
    all_to_all x1, starting transfers between devices, local(): lax.all_to_all(req_flags, 'ctx', split_axis=0, concat_axis=0, tiled=True)  13.7 us
    slice x3, local copies, waits for them, and re-layouts, joined(): tail = jax.tree.map(lambda part: part[1:], pieces)  11.8 us
    gather x1, local copies, waits for them, and re-layouts, local(): token_request.astype(jnp.bfloat16)[send_order].reshape(shards, per_peer)  10.9 us
  transfers between devices with their start and end apart: 4, of which 3 were waited for; matrix products, arithmetic and copies ran while one was open for 4% of the time, Pallas kernels for 0%

commit v1 on v0

v1 whole, which is shorter than its diff:
```python
import functools
import math

import jax
import jax.numpy as jnp
from jax import lax
from jax.experimental import pallas as pl
from jax.experimental.pallas import tpu as pltpu
from jax.sharding import PartitionSpec as P

NEG = -1e30
NX = 4
NZ = 8
CTX = NX * NZ
PER = 56
MSG = 64
LAT = 512
ROPE = 64
TOK = PER * CTX
HALF = 384
F32 = jnp.float32
BF16 = jnp.bfloat16
MESH = pl.DeviceIdType.MESH


def iota(shape, dim):
    return lax.broadcasted_iota(jnp.int32, shape, dim)


def pieces(column):
    first = column.astype(BF16).astype(F32)
    rest = column - first
    second = rest.astype(BF16).astype(F32)
    return first, second, rest - second


def pack_part(num, peak, den):
    rows = num.shape[0]
    lane = iota((rows, 128), 1)
    stats = jnp.zeros((rows, 128), F32)
    for at, column in enumerate(pieces(peak) + pieces(den)):
        stats = jnp.where(lane == at, column, stats)
    low = jnp.concatenate([num[:, HALF:], stats, jnp.zeros((rows, 128), F32)], axis=1)
    top = num[:, :HALF].reshape(rows // 8, 8, HALF)
    low = low.reshape(rows // 8, 8, HALF)
    return jnp.concatenate([top, low], axis=1).astype(BF16)


def halves(message):
    n = message.shape[0]
    value = message.astype(F32)
    top = value[:, :8, :].reshape(n * 8, HALF)
    low = value[:, 8:, :].reshape(n * 8, HALF)
    return top, low


def unpack_part(message):
    top, low = halves(message)
    num = jnp.concatenate([top, low[:, :128]], axis=1)
    peak = low[:, 128:129] + low[:, 129:130] + low[:, 130:131]
    den = low[:, 131:132] + low[:, 132:133] + low[:, 133:134]
    return num, peak, den


def join_parts(parts):
    peak = functools.reduce(jnp.maximum, [p[1] for p in parts])
    num = den = 0.0
    for one in parts:
        factor = jnp.exp(one[1] - peak)
        num = num + one[0] * factor
        den = den + one[2] * factor
    return num, peak, den


def exchange_kernel(
    scale,
    len_ref, tgt_ref, qn_ref, qr_ref, nl_ref, nr_ref, ka_ref, vu_ref, lat_hbm, rope_hbm,
    land_ref, att_ref,
    lat, rope, rope_t, pos, outbox, qz, qx, ql_s, qr_s, sc, wb, ca_src, ca_dst, cb_src, cb_dst,
    in_sem, own_sem, send_sem, recv_sem, qa_s, qa_r, qb_s, qb_r, ca_s, ca_r, cb_s, cb_r,
):
    me = lax.axis_index("ctx")
    z = me // NX
    x = lax.rem(me, NX)

    def along_z(k):
        return lax.rem(z + k, NZ)

    def along_x(k):
        return lax.rem(x + k, NX)

    load_lat = pltpu.make_async_copy(lat_hbm, lat, in_sem.at[0])
    load_rope = pltpu.make_async_copy(rope_hbm, rope, in_sem.at[1])
    load_lat.start()
    load_rope.start()

    barrier = pltpu.get_barrier_semaphore()

    def greet(i, carry):
        pl.semaphore_signal(
            barrier, inc=1, device_id={"ctx": lax.rem(me + i, CTX)}, device_id_type=MESH
        )
        return carry

    lax.fori_loop(1, CTX, greet, 0)

    qn = qn_ref[...]
    row8 = iota((8, LAT), 0)
    ql = jnp.where(
        lax.rem(row8, 2) == 0,
        jnp.dot(qn, ka_ref[0], preferred_element_type=F32),
        jnp.dot(qn, ka_ref[1], preferred_element_type=F32),
    )
    ql = ql.astype(BF16).astype(F32)
    qr = jnp.concatenate([qr_ref[...].astype(F32), jnp.zeros((8, 256 - ROPE), F32)], axis=1)
    own_query = jnp.concatenate(
        [ql[:, :HALF], jnp.concatenate([ql[:, HALF:], qr], axis=1)], axis=0
    ).astype(BF16)
    qz[z] = own_query

    shard = iota((CTX, 128), 0)
    hot = [(tgt_ref[b : b + 1, :] == shard).astype(F32) for b in range(TOK // 128)]
    before = (iota((128, 128), 0) < iota((128, 128), 1)).astype(BF16)
    prefix = jnp.dot(
        jnp.concatenate(hot, axis=0).astype(BF16), before, preferred_element_type=F32
    )
    base = (MSG * shard).astype(F32)
    for b in range(TOK // 128):
        part = hot[b]
        place = jnp.sum(part * (prefix[CTX * b : CTX * (b + 1)] + base), axis=0, keepdims=True)
        pos[0:1, 128 * b : 128 * (b + 1)] = place.astype(jnp.int32)
        base = base + jnp.sum(part, axis=1, keepdims=True)

    load_rope.wait()
    rope_t[...] = jnp.transpose(rope[...].astype(F32)).astype(BF16)
    load_lat.wait()

    def group_z(i):
        half = (i + 1) // 2
        return along_z(4 + half * (1 - 2 * lax.rem(i, 2)))

    rows = NX * MSG

    def build(i):
        first = pl.multiple_of(group_z(i) * rows, rows)
        one_hot = (pos[0:1, :] - first == iota((rows, TOK), 0)).astype(F32).astype(BF16)
        moved = jnp.dot(one_hot, lat[...], preferred_element_type=F32)
        turned = jnp.dot(one_hot, rope_t[...], preferred_element_type=F32)
        for j in range(NX):
            block = turned[MSG * j : MSG * (j + 1)]
            packed = jnp.concatenate([block[8 * k : 8 * (k + 1)] for k in range(8)], axis=1)
            whole = jnp.concatenate([moved[MSG * j : MSG * j + PER], packed], axis=0)
            outbox[pl.ds(first + MSG * j, MSG), :] = whole.astype(BF16)

    def message(i, k):
        there = group_z(i) * NX + along_x(k)
        return pltpu.make_async_remote_copy(
            src_ref=outbox.at[pl.ds(pl.multiple_of(there * MSG, MSG), MSG)],
            dst_ref=land_ref.at[pl.ds(pl.multiple_of(me * MSG, MSG), MSG)],
            send_sem=send_sem.at[there],
            recv_sem=recv_sem.at[me],
            device_id={"ctx": there},
            device_id_type=MESH,
        )

    def send(i, low=0):
        for k in range(low, NX):
            message(i, k).start()

    def build_send(i, carry):
        build(i)
        send(i)
        return carry

    def build_only(i, carry):
        build(i)
        return carry

    build(jnp.int32(0))
    pl.semaphore_wait(barrier, CTX - 1)

    def spread_z(src, dst, s_sem, r_sem, k, own):
        there = along_z(k)
        return pltpu.make_async_remote_copy(
            src_ref=src.at[z if own else there],
            dst_ref=dst.at[z],
            send_sem=s_sem.at[k],
            recv_sem=r_sem.at[k],
            device_id={"ctx": there * NX + x},
            device_id_type=MESH,
        )

    def spread_x(src, dst, s_sem, r_sem, k, own):
        there = along_x(k)
        return pltpu.make_async_remote_copy(
            src_ref=src if own else src.at[there],
            dst_ref=dst.at[x],
            send_sem=s_sem.at[k],
            recv_sem=r_sem.at[k],
            device_id={"ctx": z * NX + there},
            device_id_type=MESH,
        )

    def arrive_z(dst, r_sem, s_sem, k):
        return pltpu.make_async_remote_copy(
            src_ref=dst.at[z],
            dst_ref=dst.at[along_z(NZ - k)],
            send_sem=s_sem.at[k],
            recv_sem=r_sem.at[k],
            device_id={"ctx": along_z(k) * NX + x},
            device_id_type=MESH,
        )

    def arrive_x(dst, r_sem, s_sem, k):
        return pltpu.make_async_remote_copy(
            src_ref=dst.at[x],
            dst_ref=dst.at[along_x(NX - k)],
            send_sem=s_sem.at[k],
            recv_sem=r_sem.at[k],
            device_id={"ctx": z * NX + along_x(k)},
            device_id_type=MESH,
        )

    for k in range(1, NZ):
        spread_z(qz, qz, qa_s, qa_r, k, True).start()
    send(jnp.int32(0))
    lax.fori_loop(1, 3, build_send, 0)

    for k in range(1, NZ):
        arrive_z(qz, qa_r, qa_s, k).wait_recv()
    for k in range(1, NX):
        spread_x(qz, qx, qb_s, qb_r, k, True).start()
    qx[x] = qz[...]
    lax.fori_loop(3, 5, build_send, 0)
    lax.fori_loop(5, 8, build_only, 0)
    for k in range(1, NX):
        arrive_x(qx, qb_r, qb_s, k).wait_recv()

    for s in range(NX):
        top, low = halves(qx[s])
        ql_s[64 * s : 64 * (s + 1), :] = jnp.concatenate([top, low[:, :128]], axis=1).astype(BF16)
        qr_s[64 * s : 64 * (s + 1), :] = low[:, 128 : 128 + ROPE].astype(BF16)
    heads = 8 * CTX
    chunk = 256
    bound = len_ref[0] - me * TOK
    row_request = lax.rem(iota((heads, chunk), 0) // 2, 2)
    peak = jnp.full((heads, 1), NEG, F32)
    for c in range(TOK // chunk):
        at = slice(chunk * c, chunk * (c + 1))
        scores = lax.dot_general(
            ql_s[...], lat[at, :], (((1,), (1,)), ((), ())), preferred_element_type=F32
        ) + jnp.dot(qr_s[...], rope[:, at], preferred_element_type=F32)
        token_request = (iota((heads, chunk), 1) + chunk * c >= bound).astype(jnp.int32)
        scores = jnp.where(token_request == row_request, scores * scale, NEG)
        sc[:, at] = scores
        peak = jnp.maximum(peak, jnp.max(scores, axis=1, keepdims=True))
    den = jnp.zeros((heads, 1), F32)
    for c in range(TOK // chunk):
        at = slice(chunk * c, chunk * (c + 1))
        scores = sc[:, at]
        weight = jnp.where(scores > 0.5 * NEG, jnp.exp(scores - peak), 0.0)
        den = den + jnp.sum(weight, axis=1, keepdims=True)
        wb[:, at] = weight.astype(BF16)
    num = jnp.dot(wb[...], lat[...], preferred_element_type=F32)
    for s in range(NX):
        at = slice(64 * s, 64 * (s + 1))
        ca_src[s] = pack_part(num[at], peak[at], den[at])

    for k in range(1, NX):
        spread_x(ca_src, ca_dst, ca_s, ca_r, k, False).start()
    ca_dst[x] = ca_src[x]
    send(jnp.int32(5))
    send(jnp.int32(6))

    for k in range(1, NX):
        arrive_x(ca_dst, ca_r, ca_s, k).wait_recv()
    cb_src[...] = pack_part(*join_parts([unpack_part(ca_dst[s]) for s in range(NX)]))
    for k in range(1, NZ):
        spread_z(cb_src, cb_dst, cb_s, cb_r, k, False).start()
    cb_dst[z] = cb_src[z]
    send(jnp.int32(7), 1)
    mine = pl.ds(pl.multiple_of(me * MSG, MSG), MSG)
    keep = pltpu.make_async_copy(outbox.at[mine], land_ref.at[mine], own_sem)
    keep.start()

    top, low = halves(qz[pl.ds(z, 1)])
    own_ql = jnp.concatenate([top, low[:, :128]], axis=1)
    own_qr = low[:, 128 : 128 + ROPE]
    row_at = iota((8, 1), 0)
    fresh = []
    for f in range(4):
        key_latent = nl_ref[f : f + 1, :].astype(F32)
        key_rope = nr_ref[f : f + 1, :].astype(F32)
        score = (
            jnp.sum(own_ql * key_latent, axis=1, keepdims=True)
            + jnp.sum(own_qr * key_rope, axis=1, keepdims=True)
        ) * scale
        usable = (f // 2 <= row_at // 4) & (f % 2 == lax.rem(row_at // 2, 2))
        fresh.append((usable, jnp.where(usable, score, NEG), key_latent))

    for k in range(1, NZ):
        arrive_z(cb_dst, cb_r, cb_s, k).wait_recv()
    num, peak, den = join_parts([unpack_part(cb_dst[pl.ds(s, 1)]) for s in range(NZ)])
    top_peak = functools.reduce(jnp.maximum, [one[1] for one in fresh], peak)
    factor = jnp.exp(peak - top_peak)
    num = num * factor
    den = den * factor
    for usable, score, key_latent in fresh:
        weight = jnp.where(usable, jnp.exp(score - top_peak), 0.0)
        den = den + weight
        num = num + weight.astype(BF16).astype(F32) * key_latent
    latent_out = (num / den).astype(BF16)
    att_ref[...] = jnp.where(
        lax.rem(iota((8, 128), 0), 2) == 0,
        jnp.dot(latent_out, vu_ref[0], preferred_element_type=F32),
        jnp.dot(latent_out, vu_ref[1], preferred_element_type=F32),
    ).astype(BF16)

    def settle(i, carry):
        there = lax.rem(me + i, CTX)
        one = pltpu.make_async_remote_copy(
            src_ref=outbox.at[pl.ds(pl.multiple_of(there * MSG, MSG), MSG)],
            dst_ref=land_ref.at[pl.ds(pl.multiple_of(there * MSG, MSG), MSG)],
            send_sem=send_sem.at[there],
            recv_sem=recv_sem.at[there],
            device_id={"ctx": there},
            device_id_type=MESH,
        )
        one.wait_send()
        one.wait_recv()
        return carry

    lax.fori_loop(1, CTX, settle, 0)
    keep.wait()
    for k in range(1, NZ):
        spread_z(qz, qz, qa_s, qa_r, k, True).wait_send()
        spread_z(cb_src, cb_dst, cb_s, cb_r, k, False).wait_send()
    for k in range(1, NX):
        spread_x(qz, qx, qb_s, qb_r, k, True).wait_send()
        spread_x(ca_src, ca_dst, ca_s, ca_r, k, False).wait_send()


def unpack_kernel(land_ref, lat_ref, rope_ref):
    turned = []
    for s in range(0, land_ref.shape[0] // MSG, 2):
        both = []
        for at in (MSG * s, MSG * (s + 1)):
            value = land_ref[at : at + MSG, :].astype(F32)
            both.append(value[:PER])
            packed = value[PER:]
            turned += [packed[:, ROPE * k : ROPE * (k + 1)] for k in range(PER // 8)]
        lat_ref[PER * s : PER * (s + 2), :] = jnp.concatenate(both, axis=0).astype(BF16)
    rope_ref[...] = jnp.transpose(jnp.concatenate(turned, axis=0)).astype(BF16)


def local(
    latent_cache,
    rope_cache,
    lengths,
    target_shard,
    query_nope,
    query_rope,
    new_latent,
    new_rope,
    key_absorb,
    value_up,
):
    scale = 1.0 / math.sqrt(query_nope.shape[3] + ROPE)
    vmem = pl.BlockSpec(memory_space=pltpu.VMEM)
    anywhere = pl.BlockSpec(memory_space=pl.ANY)
    dma = pltpu.SemaphoreType.DMA
    land, attention = pl.pallas_call(
        functools.partial(exchange_kernel, scale),
        out_shape=(
            jax.ShapeDtypeStruct((CTX * MSG, LAT), BF16),
            jax.ShapeDtypeStruct((8, 128), BF16),
        ),
        in_specs=[pl.BlockSpec(memory_space=pltpu.SMEM)] + [vmem] * 7 + [anywhere] * 2,
        out_specs=(anywhere, vmem),
        scratch_shapes=[
            pltpu.VMEM((TOK, LAT), BF16),
            pltpu.VMEM((ROPE, TOK), BF16),
            pltpu.VMEM((TOK, ROPE), BF16),
            pltpu.VMEM((8, TOK), jnp.int32),
            pltpu.VMEM((CTX * MSG, LAT), BF16),
            pltpu.VMEM((NZ, 16, HALF), BF16),
            pltpu.VMEM((NX, NZ, 16, HALF), BF16),
            pltpu.VMEM((8 * CTX, LAT), BF16),
            pltpu.VMEM((8 * CTX, ROPE), BF16),
            pltpu.VMEM((8 * CTX, TOK), F32),
            pltpu.VMEM((8 * CTX, TOK), BF16),
            pltpu.VMEM((NX, NZ, 16, HALF), BF16),
            pltpu.VMEM((NX, NZ, 16, HALF), BF16),
            pltpu.VMEM((NZ, 16, HALF), BF16),
            pltpu.VMEM((NZ, 16, HALF), BF16),
            dma((2,)),
            dma,
            dma((CTX,)),
            dma((CTX,)),
            dma((NZ,)),
            dma((NZ,)),
            dma((NX,)),
            dma((NX,)),
            dma((NX,)),
            dma((NX,)),
            dma((NZ,)),
            dma((NZ,)),
        ],
        name="exchange",
        compiler_params=pltpu.CompilerParams(
            collective_id=1, has_side_effects=True, vmem_limit_bytes=40 << 20
        ),
    )(
        lengths,
        target_shard.reshape(TOK // 128, 128),
        query_nope.reshape(8, 128),
        query_rope.reshape(8, ROPE),
        new_latent.reshape(4, LAT),
        new_rope.reshape(4, ROPE),
        key_absorb,
        value_up,
        latent_cache,
        rope_cache.T,
    )
    latent_decode, rope_decode = pl.pallas_call(
        unpack_kernel,
        grid=(2,),
        out_shape=(
            jax.ShapeDtypeStruct((TOK, LAT), BF16),
            jax.ShapeDtypeStruct((ROPE, TOK), BF16),
        ),
        in_specs=[pl.BlockSpec((CTX * MSG // 2, LAT), lambda i: (i, 0))],
        out_specs=(
            pl.BlockSpec((TOK // 2, LAT), lambda i: (i, 0)),
            pl.BlockSpec((ROPE, TOK // 2), lambda i: (0, i)),
        ),
        name="unpack",
        compiler_params=pltpu.CompilerParams(vmem_limit_bytes=40 << 20),
    )(land)
    return attention.reshape(query_nope.shape), latent_decode, rope_decode.T


def solution(mesh):
    placed = (
        P(("req", "ctx"), None),
        P(("req", "ctx"), None),
        P("req"),
        P(("req", "ctx")),
        P(None, "req", "ctx", None),
        P(None, "req", "ctx", None),
        P(None, "req", None),
        P(None, "req", None),
        P("ctx", None, None),
        P("ctx", None, None),
    )
    return jax.shard_map(
        local,
        mesh=mesh,
        in_specs=placed,
        out_specs=(P(None, "req", "ctx", None), P(("req", "ctx"), None), P(("req", "ctx"), None)),
        check_vma=False,
    )
```

time: 420 us -> 81 us (0.19)
  blocking collectives: 173 us -> 0 us
  waiting for transfers between devices: 110 us -> 0 us
  Pallas kernels: 0 us -> 70.9 us
  other arithmetic: 46.2 us -> 0 us
  local copies, waits for them, and re-layouts: 40.8 us -> 9 us
  starting transfers between devices: 24.9 us -> 0 us
  between operations: 14.3 us -> 0.65 us
  matrix products: 8.49 us -> 0 us
    all_gather x4 -> x0, blocking collectives: 173 us -> none  [the longest x1 71.1 us: local(): lax.all_gather(query_rope, 'ctx', axis=2, tiled=True)]
    all_gather x1 -> x0, waiting for transfers between devices: 102 us -> none  [joined(): pieces = jax.tree.map(lambda part: lax.all_gather(part, axis), value)]
    pallas_call x0 -> x2, Pallas kernels: none -> 70.9 us  [the longest x1 69.4 us: local(): pl.pallas_call(functools.partial(exchange_kernel, scale), out_shape=(jax....]
    add x63 -> x0, other arithmetic: 38.4 us -> none  [the longest x31 37.6 us: combine_parts(): first[2] * factor_a[..., None] + second[2] * factor_b[..., None]]
    all_to_all x3 -> x0, starting transfers between devices: 24.9 us -> none  [the longest x1 13.7 us: local(): lax.all_to_all(req_flags, 'ctx', split_axis=0, concat_axis=0, tiled=True)]
    gather x3 -> x0, local copies, waits for them, and re-layouts: 20.8 us -> none  [the longest x1 10.9 us: local(): token_request.astype(jnp.bfloat16)[send_order].reshape(shards, per_peer)]
    slice x3 -> x0, local copies, waits for them, and re-layouts: 11.8 us -> none  [joined(): tail = jax.tree.map(lambda part: part[1:], pieces)]
    dot_general x8 -> x0, matrix products: 8.49 us -> none  [the longest x4 4.9 us: contract(): lax.dot_general(left, right, (((1,), (1,)), ((), ())), preferred_element_...]
  transfers between devices with their start and end apart: 4 -> 0, of which waited for: 3 -> 0; matrix products, arithmetic and copies ran while one was open for 4% -> 0% of each run, Pallas kernels for 0% -> 0%
where the time goes in v1:
time: 81 us; the launch traced here: 80.6 us
  Pallas kernels  70.9 us (88%)
  local copies, waits for them, and re-layouts  9 us (11%)
    pallas_call x1, Pallas kernels, local(): pl.pallas_call(functools.partial(exchange_kernel, scale), out_shape=(jax....  69.4 us
    unnamed x19, local copies, waits for them, and re-layouts  8.3 us

profile of v1, /device:TPU:1, one launch (start us, length us, event | category | flops | bytes accessed | tf_op | source)
XLA Modules:
  0.0 80.6 jit_solution(7064768628815941581)
XLA Ops:
  0.6 0.7 reshape.27.nl_ref
  1.3 0.0 copy-start
  1.3 1.5 %copy-done = bf16[1792,512]{1,0:T(8,128)(2,1)S(1)} copy-done((bf16[1792,512]{1,0:T(8,128)(2,1)S(1)}, bf16[1792,512]{1,0:T(8,128)(2,1)}, u32[]{:S(2)}) %copy-start) | copy-done | bytes 1835032
  2.8 0.0 copy-start.1
  2.8 0.9 %copy-done.1 = bf16[2,128,512]{2,1,0:T(8,128)(2,1)S(1)} copy-done((bf16[2,128,512]{2,1,0:T(8,128)(2,1)S(1)}, bf16[2,128,512]{2,1,0:T(8,128)(2,1)}, u32[]{:S(2)}) %copy-start.1) | copy-done | bytes 262168
  3.8 0.0 copy-start.2
  3.8 0.9 %copy-done.2 = bf16[2,512,128]{2,1,0:T(8,128)(2,1)S(1)} copy-done((bf16[2,512,128]{2,1,0:T(8,128)(2,1)S(1)}, bf16[2,512,128]{2,1,0:T(8,128)(2,1)}, u32[]{:S(2)}) %copy-start.2) | copy-done | bytes 262168
  4.7 0.0 copy-start.3
  4.7 0.9 %copy-done.3 = bf16[1792,64]{0,1:T(8,128)(2,1)S(1)} copy-done((bf16[1792,64]{0,1:T(8,128)(2,1)S(1)}, bf16[1792,64]{0,1:T(8,128)(2,1)}, u32[]{:S(2)}) %copy-start.3) | copy-done | bytes 229400
  5.7 0.0 copy-start.4
  5.7 0.7 copy-done.4
  6.4 0.0 copy-start.5
  6.4 0.7 copy-done.5
  7.0 0.0 copy-start.6
  7.0 0.7 copy-done.6
  7.7 0.0 copy-start.7
  7.7 0.7 copy-done.7
  8.4 0.0 copy-start.8
  8.4 0.7 copy-done.8
  9.1 69.4 %exchange.1 = (bf16[2048,512]{1,0:T(8,128)(2,1)S(1)}, bf16[8,128]{1,0:T(8,128)(2,1)S(1)}) custom-call(s32[2]{0:T(128)S(1)} %copy-done.8, s32[14,128]{1,0:T(8,128)S(1)} %bitcast.8, bf16[8,128]{1,0:T(8,128)(2,1)S(1)} %bitcast.10, bf16[8,64]{1,0:T(8,128)(2,1)S(1)} %bitcast.11, bf16[4,512]{1,0:T(4,128)(2,1)S(1)} %reshape.27.nl_ref, bf16[4,64]{1,0:T(4,128)(2,1)S(1)} %bitcast.12, ...), custom_call_target="tpu_custom_call" | custom-call | tf_op jit(solution)/shard_map/exchange/pallas_call | solution.py:372
  78.5 1.5 %unpack.1 = (bf16[1792,512]{1,0:T(8,128)(2,1)}, bf16[64,1792]{1,0:T(8,128)(2,1)}) custom-call(bf16[2048,512]{1,0:T(8,128)(2,1)S(1)} %get-tuple-element.8.land_ref), custom_call_target="tpu_custom_call" | custom-call | tf_op jit(solution)/shard_map/unpack/pallas_call | solution.py:425
  80.0 0.6 copy.14
Async XLA Ops:
  1.3 1.5 %copy-start = (bf16[1792,512]{1,0:T(8,128)(2,1)S(1)}, bf16[1792,512]{1,0:T(8,128)(2,1)}, u32[]{:S(2)}) copy-start(bf16[1792,512]{1,0:T(8,128)(2,1)} %lat_hbm.1) | copy-start | bytes 5505028
  2.8 0.9 %copy-start.1 = (bf16[2,128,512]{2,1,0:T(8,128)(2,1)S(1)}, bf16[2,128,512]{2,1,0:T(8,128)(2,1)}, u32[]{:S(2)}) copy-start(bf16[2,128,512]{2,1,0:T(8,128)(2,1)} %ka_ref.1) | copy-start | bytes 786436
  3.8 0.9 %copy-start.2 = (bf16[2,512,128]{2,1,0:T(8,128)(2,1)S(1)}, bf16[2,512,128]{2,1,0:T(8,128)(2,1)}, u32[]{:S(2)}) copy-start(bf16[2,512,128]{2,1,0:T(8,128)(2,1)} %vu_ref.1) | copy-start | bytes 786436
  4.7 0.9 %copy-start.3 = (bf16[1792,64]{0,1:T(8,128)(2,1)S(1)}, bf16[1792,64]{0,1:T(8,128)(2,1)}, u32[]{:S(2)}) copy-start(bf16[1792,64]{0,1:T(8,128)(2,1)} %param.11) | copy-start | bytes 688132
  5.7 0.7 copy-start.4
  6.4 0.7 copy-start.5
  7.0 0.7 copy-start.6
  7.7 0.7 copy-start.7
  8.4 0.7 copy-start.8

commit v2 on v1

--- a/solution.py
+++ b/solution.py
@@ -74,9 +74,9 @@
 
 def exchange_kernel(
     scale,
-    len_ref, tgt_ref, qn_ref, qr_ref, nl_ref, nr_ref, ka_ref, vu_ref, lat_hbm, rope_hbm,
+    tgt_hbm, ka_hbm, qn_hbm, qr_hbm, rope_hbm, lat_hbm, len_hbm, nl_hbm, nr_hbm, vu_hbm,
     land_ref, att_ref,
-    lat, rope, rope_t, pos, outbox, qz, qx, ql_s, qr_s, sc, wb, ca_src, ca_dst, cb_src, cb_dst,
+    tgt_ref, ka_ref, qn_ref, qr_ref, rope, lat, len_ref, nl_ref, nr_ref, vu_ref, rope_t, pos, outbox, qz, qx, ql_s, qr_s, sc, wb, ca_src, ca_dst, cb_src, cb_dst,
     in_sem, own_sem, send_sem, recv_sem, qa_s, qa_r, qb_s, qb_r, ca_s, ca_r, cb_s, cb_r,
 ):
     me = lax.axis_index("ctx")
@@ -89,10 +89,25 @@
     def along_x(k):
         return lax.rem(x + k, NX)
 
-    load_lat = pltpu.make_async_copy(lat_hbm, lat, in_sem.at[0])
-    load_rope = pltpu.make_async_copy(rope_hbm, rope, in_sem.at[1])
-    load_lat.start()
-    load_rope.start()
+    loads = [
+        pltpu.make_async_copy(src, dst, in_sem.at[i])
+        for i, (src, dst) in enumerate(
+            (
+                (tgt_hbm, tgt_ref),
+                (ka_hbm, ka_ref),
+                (qn_hbm, qn_ref),
+                (qr_hbm, qr_ref),
+                (rope_hbm, rope),
+                (lat_hbm, lat),
+                (len_hbm, len_ref),
+                (nl_hbm, nl_ref),
+                (nr_hbm, nr_ref),
+                (vu_hbm, vu_ref),
+            )
+        )
+    ]
+    for load in loads:
+        load.start()
 
     barrier = pltpu.get_barrier_semaphore()
 
@@ -104,6 +119,8 @@
 
     lax.fori_loop(1, CTX, greet, 0)
 
+    for load in loads[1:4]:
+        load.wait()
     qn = qn_ref[...]
     row8 = iota((8, LAT), 0)
     ql = jnp.where(
@@ -118,6 +135,7 @@
     ).astype(BF16)
     qz[z] = own_query
 
+    loads[0].wait()
     shard = iota((CTX, 128), 0)
     hot = [(tgt_ref[b : b + 1, :] == shard).astype(F32) for b in range(TOK // 128)]
     before = (iota((128, 128), 0) < iota((128, 128), 1)).astype(BF16)
@@ -131,9 +149,9 @@
         pos[0:1, 128 * b : 128 * (b + 1)] = place.astype(jnp.int32)
         base = base + jnp.sum(part, axis=1, keepdims=True)
 
-    load_rope.wait()
+    loads[4].wait()
     rope_t[...] = jnp.transpose(rope[...].astype(F32)).astype(BF16)
-    load_lat.wait()
+    loads[5].wait()
 
     def group_z(i):
         half = (i + 1) // 2
@@ -242,6 +260,7 @@
         qr_s[64 * s : 64 * (s + 1), :] = low[:, 128 : 128 + ROPE].astype(BF16)
     heads = 8 * CTX
     chunk = 256
+    loads[6].wait()
     bound = len_ref[0] - me * TOK
     row_request = lax.rem(iota((heads, chunk), 0) // 2, 2)
     peak = jnp.full((heads, 1), NEG, F32)
@@ -288,9 +307,11 @@
     own_qr = low[:, 128 : 128 + ROPE]
     row_at = iota((8, 1), 0)
     fresh = []
+    for load in loads[7:]:
+        load.wait()
     for f in range(4):
-        key_latent = nl_ref[f : f + 1, :].astype(F32)
-        key_rope = nr_ref[f : f + 1, :].astype(F32)
+        key_latent = nl_ref[f // 2].astype(F32)[f % 2 : f % 2 + 1, :]
+        key_rope = nr_ref[f // 2].astype(F32)[f % 2 : f % 2 + 1, :]
         score = (
             jnp.sum(own_ql * key_latent, axis=1, keepdims=True)
             + jnp.sum(own_qr * key_rope, axis=1, keepdims=True)
@@ -340,7 +361,8 @@
         spread_x(ca_src, ca_dst, ca_s, ca_r, k, False).wait_send()
 
 
-def unpack_kernel(land_ref, lat_ref, rope_ref):
+def unpack_kernel(land_ref, part_ref, lat_ref, rope_ref, att_ref):
+    att_ref[...] = part_ref[...]
     turned = []
     for s in range(0, land_ref.shape[0] // MSG, 2):
         both = []
@@ -367,19 +389,28 @@
 ):
     scale = 1.0 / math.sqrt(query_nope.shape[3] + ROPE)
     vmem = pl.BlockSpec(memory_space=pltpu.VMEM)
+    hbm = pl.BlockSpec(memory_space=pltpu.HBM)
     anywhere = pl.BlockSpec(memory_space=pl.ANY)
     dma = pltpu.SemaphoreType.DMA
     land, attention = pl.pallas_call(
         functools.partial(exchange_kernel, scale),
         out_shape=(
-            jax.ShapeDtypeStruct((CTX * MSG, LAT), BF16),
-            jax.ShapeDtypeStruct((8, 128), BF16),
+            pltpu.VMEM((CTX * MSG, LAT), BF16),
+            pltpu.VMEM((8, 128), BF16),
         ),
-        in_specs=[pl.BlockSpec(memory_space=pltpu.SMEM)] + [vmem] * 7 + [anywhere] * 2,
+        in_specs=[hbm] * 10,
         out_specs=(anywhere, vmem),
         scratch_shapes=[
+            pltpu.VMEM((TOK // 128, 128), jnp.int32),
+            pltpu.VMEM(key_absorb.shape, BF16),
+            pltpu.VMEM((8, 128), BF16),
+            pltpu.VMEM((8, ROPE), BF16),
+            pltpu.VMEM((ROPE, TOK), BF16),
             pltpu.VMEM((TOK, LAT), BF16),
-            pltpu.VMEM((ROPE, TOK), BF16),
+            pltpu.SMEM((2,), jnp.int32),
+            pltpu.VMEM(new_latent.shape, BF16),
+            pltpu.VMEM(new_rope.shape, BF16),
+            pltpu.VMEM(value_up.shape, BF16),
             pltpu.VMEM((TOK, ROPE), BF16),
             pltpu.VMEM((8, TOK), jnp.int32),
             pltpu.VMEM((CTX * MSG, LAT), BF16),
@@ -393,7 +424,7 @@
             pltpu.VMEM((NX, NZ, 16, HALF), BF16),
             pltpu.VMEM((NZ, 16, HALF), BF16),
             pltpu.VMEM((NZ, 16, HALF), BF16),
-            dma((2,)),
+            dma((10,)),
             dma,
             dma((CTX,)),
             dma((CTX,)),
@@ -411,32 +442,39 @@
             collective_id=1, has_side_effects=True, vmem_limit_bytes=40 << 20
         ),
     )(
-        lengths,
-        target_shard.reshape(TOK // 128, 128),
-        query_nope.reshape(8, 128),
-        query_rope.reshape(8, ROPE),
-        new_latent.reshape(4, LAT),
-        new_rope.reshape(4, ROPE),
-        key_absorb,
-        value_up,
-        latent_cache,
-        rope_cache.T,
+        *(pltpu.with_memory_space_constraint(array, pltpu.HBM) for array in (
+            target_shard.reshape(TOK // 128, 128),
+            key_absorb,
+            query_nope.reshape(8, 128),
+            query_rope.reshape(8, ROPE),
+            rope_cache.T,
+            latent_cache,
+            lengths,
+            new_latent,
+            new_rope,
+            value_up,
+        ))
     )
-    latent_decode, rope_decode = pl.pallas_call(
+    latent_decode, rope_decode, attention = pl.pallas_call(
         unpack_kernel,
         grid=(2,),
         out_shape=(
             jax.ShapeDtypeStruct((TOK, LAT), BF16),
             jax.ShapeDtypeStruct((ROPE, TOK), BF16),
+            jax.ShapeDtypeStruct((8, 128), BF16),
         ),
-        in_specs=[pl.BlockSpec((CTX * MSG // 2, LAT), lambda i: (i, 0))],
+        in_specs=[
+            pl.BlockSpec((CTX * MSG // 2, LAT), lambda i: (i, 0)),
+            pl.BlockSpec((8, 128), lambda i: (0, 0)),
+        ],
         out_specs=(
             pl.BlockSpec((TOK // 2, LAT), lambda i: (i, 0)),
             pl.BlockSpec((ROPE, TOK // 2), lambda i: (0, i)),
+            pl.BlockSpec((8, 128), lambda i: (0, 0)),
         ),
         name="unpack",
-        compiler_params=pltpu.CompilerParams(vmem_limit_bytes=40 << 20),
-    )(land)
+        compiler_params=pltpu.CompilerParams(vmem_limit_bytes=24 << 20),
+    )(land, attention)
     return attention.reshape(query_nope.shape), latent_decode, rope_decode.T
 
 

time: 81 us -> 70.8 us (0.87)
  local copies, waits for them, and re-layouts: 9 us -> 0 us
  Pallas kernels: 70.9 us -> 70 us
    unnamed x19 -> x0, local copies, waits for them, and re-layouts: 8.3 us -> none
    pallas_call x1, Pallas kernels: 69.4 us -> 68.5 us  [local(): pl.pallas_call(functools.partial(exchange_kernel, scale), out_shape=(pltp...]
where the time goes in v2:
time: 70.8 us; the launch traced here: 70.7 us
  Pallas kernels  70 us (99%)
    pallas_call x1, Pallas kernels, local(): pl.pallas_call(functools.partial(exchange_kernel, scale), out_shape=(pltp...  68.5 us
    pallas_call x1, Pallas kernels, local(): pl.pallas_call(unpack_kernel, grid=(2,), out_shape=(jax.ShapeDtypeStruct(...  1.49 us

profile of v2, /device:TPU:1, one launch (start us, length us, event | category | flops | bytes accessed | tf_op | source)
XLA Modules:
  0.0 70.7 jit_solution(17911799626371777445)
XLA Ops:
  0.6 68.5 %exchange.1 = (bf16[2048,512]{1,0:T(8,128)(2,1)S(1)}, bf16[8,128]{1,0:T(8,128)(2,1)S(1)}) custom-call(s32[14,128]{1,0:T(8,128)} %bitcast.7, bf16[2,128,512]{2,1,0:T(8,128)(2,1)} %ka_hbm.1, bf16[8,128]{1,0:T(8,128)(2,1)} %bitcast.8, bf16[8,64]{1,0:T(8,128)(2,1)} %bitcast.9, bf16[64,1792]{1,0:T(8,128)(2,1)} %bitcast.6, bf16[1792,512]{1,0:T(8,128)(2,1)} %lat_hbm.1, ...), custom_call_target="tpu_custom_call" | custom-call | tf_op jit(solution)/shard_map/exchange/pallas_call | solution.py:395
  69.2 1.5 %unpack.1 = (bf16[1792,512]{1,0:T(8,128)(2,1)}, bf16[64,1792]{1,0:T(8,128)(2,1)}, bf16[8,128]{1,0:T(8,128)(2,1)}) custom-call(bf16[2048,512]{1,0:T(8,128)(2,1)S(1)} %get-tuple-element.8.land_ref, bf16[8,128]{1,0:T(8,128)(2,1)S(1)} %get-tuple-element.9.part_ref), custom_call_target="tpu_custom_call" | custom-call | tf_op jit(solution)/shard_map/unpack/pallas_call | solution.py:458

commit v3 on v2

--- a/solution.py
+++ b/solution.py
@@ -84,7 +84,7 @@
     x = lax.rem(me, NX)
 
     def along_z(k):
-        return lax.rem(z + k, NZ)
+        return lax.rem(z + k + NZ, NZ)
 
     def along_x(k):
         return lax.rem(x + k, NX)
@@ -153,25 +153,28 @@
     rope_t[...] = jnp.transpose(rope[...].astype(F32)).astype(BF16)
     loads[5].wait()
 
-    def group_z(i):
-        half = (i + 1) // 2
-        return along_z(4 + half * (1 - 2 * lax.rem(i, 2)))
+    def shard_of(i, k):
+        step = (i + 1) // 2 * (2 * lax.rem(i, 2) - 1) + 2 * k
+        return lax.rem(z + step + NZ, NZ) * NX + along_x(k)
 
     rows = NX * MSG
 
     def build(i):
-        first = pl.multiple_of(group_z(i) * rows, rows)
-        one_hot = (pos[0:1, :] - first == iota((rows, TOK), 0)).astype(F32).astype(BF16)
+        row = iota((rows, 1), 0)
+        place = lax.rem(row, MSG)
+        for k in range(NX):
+            place = place + jnp.where(row // MSG == k, MSG * shard_of(i, k), 0)
+        one_hot = (pos[0:1, :] == place).astype(F32).astype(BF16)
         moved = jnp.dot(one_hot, lat[...], preferred_element_type=F32)
         turned = jnp.dot(one_hot, rope_t[...], preferred_element_type=F32)
         for j in range(NX):
             block = turned[MSG * j : MSG * (j + 1)]
             packed = jnp.concatenate([block[8 * k : 8 * (k + 1)] for k in range(8)], axis=1)
             whole = jnp.concatenate([moved[MSG * j : MSG * j + PER], packed], axis=0)
-            outbox[pl.ds(first + MSG * j, MSG), :] = whole.astype(BF16)
+            outbox[pl.ds(pl.multiple_of(MSG * shard_of(i, j), MSG), MSG), :] = whole.astype(BF16)
 
     def message(i, k):
-        there = group_z(i) * NX + along_x(k)
+        there = shard_of(i, k)
         return pltpu.make_async_remote_copy(
             src_ref=outbox.at[pl.ds(pl.multiple_of(there * MSG, MSG), MSG)],
             dst_ref=land_ref.at[pl.ds(pl.multiple_of(me * MSG, MSG), MSG)],
@@ -188,10 +191,6 @@
     def build_send(i, carry):
         build(i)
         send(i)
-        return carry
-
-    def build_only(i, carry):
-        build(i)
         return carry
 
     build(jnp.int32(0))
@@ -241,7 +240,7 @@
 
     for k in range(1, NZ):
         spread_z(qz, qz, qa_s, qa_r, k, True).start()
-    send(jnp.int32(0))
+    send(jnp.int32(0), 1)
     lax.fori_loop(1, 3, build_send, 0)
 
     for k in range(1, NZ):
@@ -249,8 +248,7 @@
     for k in range(1, NX):
         spread_x(qz, qx, qb_s, qb_r, k, True).start()
     qx[x] = qz[...]
-    lax.fori_loop(3, 5, build_send, 0)
-    lax.fori_loop(5, 8, build_only, 0)
+    lax.fori_loop(3, 8, build_send, 0)
     for k in range(1, NX):
         arrive_x(qx, qb_r, qb_s, k).wait_recv()
 
@@ -288,8 +286,6 @@
     for k in range(1, NX):
         spread_x(ca_src, ca_dst, ca_s, ca_r, k, False).start()
     ca_dst[x] = ca_src[x]
-    send(jnp.int32(5))
-    send(jnp.int32(6))
 
     for k in range(1, NX):
         arrive_x(ca_dst, ca_r, ca_s, k).wait_recv()
@@ -297,7 +293,6 @@
     for k in range(1, NZ):
         spread_z(cb_src, cb_dst, cb_s, cb_r, k, False).start()
     cb_dst[z] = cb_src[z]
-    send(jnp.int32(7), 1)
     mine = pl.ds(pl.multiple_of(me * MSG, MSG), MSG)
     keep = pltpu.make_async_copy(outbox.at[mine], land_ref.at[mine], own_sem)
     keep.start()

time: 70.8 us -> 68.8 us (0.972)
  Pallas kernels: 70 us -> 67.7 us
    pallas_call x1, Pallas kernels: 68.5 us -> 66.2 us  [local(): pl.pallas_call(functools.partial(exchange_kernel, scale), out_shape=(pltp...]
where the time goes in v3:
time: 68.8 us; the launch traced here: 68.4 us
  Pallas kernels  67.7 us (98%)
    pallas_call x1, Pallas kernels, local(): pl.pallas_call(functools.partial(exchange_kernel, scale), out_shape=(pltp...  66.2 us
    pallas_call x1, Pallas kernels, local(): pl.pallas_call(unpack_kernel, grid=(2,), out_shape=(jax.ShapeDtypeStruct(...  1.49 us

profile of v3, /device:TPU:1, one launch (start us, length us, event | category | flops | bytes accessed | tf_op | source)
XLA Modules:
  0.0 68.4 jit_solution(16075538234028146351)
XLA Ops:
  0.6 66.2 %exchange.1 = (bf16[2048,512]{1,0:T(8,128)(2,1)S(1)}, bf16[8,128]{1,0:T(8,128)(2,1)S(1)}) custom-call(s32[14,128]{1,0:T(8,128)} %bitcast.7, bf16[2,128,512]{2,1,0:T(8,128)(2,1)} %ka_hbm.1, bf16[8,128]{1,0:T(8,128)(2,1)} %bitcast.8, bf16[8,64]{1,0:T(8,128)(2,1)} %bitcast.9, bf16[64,1792]{1,0:T(8,128)(2,1)} %bitcast.6, bf16[1792,512]{1,0:T(8,128)(2,1)} %lat_hbm.1, ...), custom_call_target="tpu_custom_call" | custom-call | tf_op jit(solution)/shard_map/exchange/pallas_call | solution.py:390
  66.9 1.5 %unpack.1 = (bf16[1792,512]{1,0:T(8,128)(2,1)}, bf16[64,1792]{1,0:T(8,128)(2,1)}, bf16[8,128]{1,0:T(8,128)(2,1)}) custom-call(bf16[2048,512]{1,0:T(8,128)(2,1)S(1)} %get-tuple-element.8.land_ref, bf16[8,128]{1,0:T(8,128)(2,1)S(1)} %get-tuple-element.9.part_ref), custom_call_target="tpu_custom_call" | custom-call | tf_op jit(solution)/shard_map/unpack/pallas_call | solution.py:453
